TPU v7x, 32 devices: a whole 2x2x4 slice. The times are simulated.
32 devices in a mesh: ty: 4 (over x, core), tx: 8 (over z, y).
Axes of the slice: x: 2, y: 2, z: 4, core: 2. Of those that a mesh axis runs over, the one named last changes fastest.
Arguments:
- features: bfloat16 [128, 256, 512], P('ty', 'tx'), may hold values from -6 to 6
- block_reduce: bfloat16 [2, 512, 128], replicated, may hold values from -0.375 to 0.375
- block_spatial: bfloat16 [2, 9, 128, 128], replicated, may hold values from -0.25 to 0.25
- block_expand: bfloat16 [2, 128, 512], replicated, may hold values from -0.5 to 0.5
- mask_first: bfloat16 [9, 512, 256], replicated, may hold values from -0.125 to 0.125
- mask_rest: bfloat16 [3, 9, 256, 256], replicated, may hold values from -0.1875 to 0.1875
- mask_logit: bfloat16 [256], replicated, may hold values from -0.5 to 0.5
- box_reduce: bfloat16 [512, 128], replicated, may hold values from -0.25 to 0.25
- box_hidden: bfloat16 [6272, 1024], replicated, may hold values from -0.109375 to 0.109375
- box_second: bfloat16 [1024, 1024], replicated, may hold values from -0.25 to 0.25
- box_predict: bfloat16 [1024, 5], replicated, may hold values from -0.25 to 0.25
- roi_anchor: int32 [4, 8, 32, 2], P('ty', 'tx'), may hold values from 0 to 18
- roi_dest: int32 [4, 8, 32], P('ty', 'tx'), may hold values from -1 to 7, as said below
- roi_slot: int32 [4, 8, 32], P('ty', 'tx'), may hold values from -1 to 15, as said below
Outputs:
- section_features: bfloat16 [128, 256, 512], P('ty', 'tx')
- mask_logits: float32 [4, 8, 32, 196], P('ty', 'tx')
- box_scores: float32 [4, 8, 32, 5], P('ty', 'tx')
Inputs may be any that keep to these rules, and one draw needn't show every extreme that they name: `roi_dest`: -1 marks an unused slot; used slots of a tile come first; in each row of tiles every head column receives exactly 16 ROIs; used slots of one tile with the same value lie a multiple of 8 positions apart. -1 exactly where roi_dest is -1; within one row of tiles no two used slots share both roi_dest and roi_slot.
All inputs are finite; a program needn't handle non-finite values.
Results may differ from a plain program's by a relative error of at most 0.033.
Values may be sent and summed in bfloat16 or wider, within the bound.
A program may use at most 128 MiB of HBM per device.

v0:
```python
import jax
import jax.numpy as jnp
import numpy as np
from jax import lax
from jax.experimental import pallas as pl
from jax.experimental.pallas import tpu as pltpu
from jax.sharding import PartitionSpec as P

CROP = 14
SIDE = 32
WIDE = 48
F32 = jnp.float32
BF16 = jnp.bfloat16

DIRS = ((-1, 0), (1, 0), (0, -1), (0, 1), (-1, -1), (-1, 1), (1, -1), (1, 1))
SLOTS = ((0, 64), (64, 64), (128, 64), (192, 64), (256, 16), (272, 16), (288, 16), (304, 16))
EDGE_ROWS = 320


def pack_matrix():
    chosen = np.zeros((192, SIDE * SIDE), np.float32)
    row = 0
    for cols in ((0, 1), (30, 31)):
        for r in range(SIDE):
            for c in cols:
                chosen[row, r * SIDE + c] = 1
                row += 1
    for at, (rows, cols) in enumerate(
        (((0, 1), (0, 1)), ((0, 1), (30, 31)), ((30, 31), (0, 1)), ((30, 31), (30, 31)))
    ):
        for a, r in enumerate(rows):
            for b, c in enumerate(cols):
                chosen[128 + 16 * at + 2 * a + b, r * SIDE + c] = 1
    return chosen


def side_matrix():
    chosen = np.zeros((37, 16, EDGE_ROWS), np.float32)
    for k in range(37):
        for q in (0, 1, 14, 15):
            right = q < 2
            r = k - 3 if right else k - 2
            b = q if right else q - 14
            if r < -2 or r > 33:
                continue
            if r < 0:
                start = (272 if right else 256) + 2 * (r + 2)
            elif r < SIDE:
                start = (192 if right else 128) + 2 * r
            else:
                start = (304 if right else 288) + 2 * (r - SIDE)
            chosen[k, q, start + b] = 1
    return chosen.reshape(37 * 16, EDGE_ROWS)


def halo_kernel(rows_total, cols_total, feat, pack, edges, packed, send_sem, recv_sem):
    row, col = lax.axis_index("ty"), lax.axis_index("tx")

    def exists(step):
        down, across = step
        there = jnp.bool_(True)
        if down:
            there = (row > 0) if down < 0 else (row < rows_total - 1)
        if across:
            side = (col > 0) if across < 0 else (col < cols_total - 1)
            there = jnp.logical_and(there, side) if down else side
        return there

    def target(step):
        return (row + step[0], col + step[1])

    barrier = pltpu.get_barrier_semaphore()
    count = jnp.int32(0)
    for step in DIRS:
        there = exists(step)
        count = count + there.astype(jnp.int32)

        @pl.when(there)
        def _():
            pl.semaphore_signal(
                barrier, inc=1, device_id=target(step), device_id_type=pl.DeviceIdType.MESH
            )

    packed[...] = jnp.dot(pack[...], feat[...], preferred_element_type=F32).astype(BF16)
    pl.semaphore_wait(barrier, count)

    sources = (
        feat.at[pl.ds(0, 64)],
        feat.at[pl.ds(960, 64)],
        packed.at[pl.ds(0, 64)],
        packed.at[pl.ds(64, 64)],
        packed.at[pl.ds(128, 16)],
        packed.at[pl.ds(144, 16)],
        packed.at[pl.ds(160, 16)],
        packed.at[pl.ds(176, 16)],
    )

    def copy_of(at):
        step = DIRS[at]
        back = DIRS.index((-step[0], -step[1]))
        start, size = SLOTS[back]
        return pltpu.make_async_remote_copy(
            src_ref=sources[at],
            dst_ref=edges.at[pl.ds(start, size)],
            send_sem=send_sem.at[at],
            recv_sem=recv_sem.at[back],
            device_id=target(step),
            device_id_type=pl.DeviceIdType.MESH,
        )

    def arrival_of(at):
        start, size = SLOTS[at]
        slot = edges.at[pl.ds(start, size)]
        return pltpu.make_async_remote_copy(
            src_ref=slot,
            dst_ref=slot,
            send_sem=send_sem.at[at],
            recv_sem=recv_sem.at[at],
            device_id=target(DIRS[at]),
            device_id_type=pl.DeviceIdType.MESH,
        )

    for at, step in enumerate(DIRS):

        @pl.when(exists(step))
        def _():
            copy_of(at).start()

        @pl.when(jnp.logical_not(exists(step)))
        def _():
            start, size = SLOTS[at]
            edges[pl.ds(start, size)] = jnp.zeros((size, edges.shape[1]), BF16)

    for at, step in enumerate(DIRS):

        @pl.when(exists(step))
        def _():
            copy_of(at).wait_send()
            arrival_of(at).wait_recv()


def exchange(features, rows_total, cols_total):
    chans = features.shape[1]
    vmem = pl.BlockSpec(memory_space=pltpu.VMEM)
    return pl.pallas_call(
        lambda *refs: halo_kernel(rows_total, cols_total, *refs),
        out_shape=jax.ShapeDtypeStruct((EDGE_ROWS, chans), BF16),
        in_specs=[vmem, vmem],
        out_specs=vmem,
        scratch_shapes=[
            pltpu.VMEM((192, chans), BF16),
            pltpu.SemaphoreType.DMA((8,)),
            pltpu.SemaphoreType.DMA((8,)),
        ],
        compiler_params=pltpu.CompilerParams(
            collective_id=0, has_side_effects=True, vmem_limit_bytes=16 * 2**20
        ),
    )(features, jnp.asarray(pack_matrix(), BF16))


def dot(left, right):
    return jnp.dot(left, right, preferred_element_type=F32)


def shifted(first, middle, last):
    total = first.shape[0]
    return pltpu.roll(first, 1, 0) + middle + pltpu.roll(last, total - 1, 0)


def conv_rows(rows_of, weight_of):
    lhs = jnp.concatenate([rows_of(i) for i in range(3)], axis=1)
    return [
        dot(lhs, jnp.concatenate([weight_of(3 * i + j) for i in range(3)], axis=0))
        for j in range(3)
    ]


GROUP = 4


def main_kernel(
    rows_total,
    cols_total,
    anchor,
    feat,
    edges,
    side,
    reduce_w,
    spatial_w,
    expand_w,
    first_hbm,
    rest_hbm,
    logit_w,
    box_reduce,
    hidden_hbm,
    second_hbm,
    predict_w,
    out_map,
    out_logits,
    out_scores,
    first_w,
    rest_w,
    hidden_w,
    second_w,
    wide,
    inner,
    wide_next,
    tile,
    variants,
    pooled,
    box_in,
    box_sum,
    crop_a,
    crop_b,
    sems,
):
    copies = [
        pltpu.make_async_copy(source, place, sems.at[at])
        for at, (source, place) in enumerate(
            ((first_hbm, first_w), (rest_hbm, rest_w), (hidden_hbm, hidden_w), (second_hbm, second_w))
        )
    ]
    for copy in copies:
        copy.start()
    chans = feat.shape[1]
    row_at, col_at = lax.axis_index("ty"), lax.axis_index("tx")

    ring = dot(side[...], edges[...]).astype(BF16)
    wide[:, 32:48, :] = ring.reshape(37, 16, chans)
    wide[3:35, 0:32, :] = feat[...].reshape(32, 32, chans)
    wide[0:1, 0:32, :] = jnp.zeros((1, 32, chans), BF16)
    wide[1:3, 0:32, :] = edges[0:64, :].reshape(2, 32, chans)
    wide[35:37, 0:32, :] = edges[64:128, :].reshape(2, 32, chans)

    width = reduce_w.shape[2]
    inner[...] = (
        jnp.maximum(dot(wide[...].reshape(37 * WIDE, chans), reduce_w[0]), 0)
        .astype(BF16)
        .reshape(37, WIDE, width)
    )
    parts = conv_rows(
        lambda i: inner[i : i + 35].reshape(35 * WIDE, width), lambda o: spatial_w[0, o]
    )
    spatial = jnp.maximum(shifted(*parts), 0).astype(BF16)
    grown = jnp.maximum(
        wide[1:36].reshape(35 * WIDE, chans).astype(F32) + dot(spatial, expand_w[0]), 0
    ).astype(BF16)
    wide_next[...] = grown.reshape(35, WIDE, chans)

    k_at = lax.broadcasted_iota(jnp.int32, (35, WIDE, width), 0) + 1
    p_at = lax.broadcasted_iota(jnp.int32, (35, WIDE, width), 1)
    is_left = p_at >= 40
    r_at = jnp.where(is_left, k_at - 2, k_at - 3)
    low_r = jnp.where(row_at == 0, 0, -8)
    high_r = jnp.where(row_at == rows_total - 1, 31, 64)
    left_ok = col_at > 0
    high_c = jnp.where(col_at == cols_total - 1, 31, 64)
    low_p = jnp.where(left_ok, 64, 40)
    keep = (r_at >= low_r) & (r_at <= high_r) & (p_at < low_p)
    keep = keep & (is_left | (p_at <= high_c))
    inner_next = jnp.maximum(dot(grown, reduce_w[1]), 0).reshape(35, WIDE, width)
    inner[0:35] = jnp.where(keep, inner_next, 0.0).astype(BF16)
    parts = conv_rows(
        lambda i: inner[i : i + 33].reshape(33 * WIDE, width), lambda o: spatial_w[1, o]
    )
    spatial = jnp.maximum(shifted(*parts), 0).reshape(33, WIDE, width)
    spatial = spatial[1:33, 0:32].reshape(1024, width).astype(BF16)
    result = jnp.maximum(
        wide_next[2:34, 0:32].reshape(1024, chans).astype(F32) + dot(spatial, expand_w[1]), 0
    ).astype(BF16)
    out_map[...] = result
    tile[1:33] = result.reshape(32, 32, chans)
    tile[0:1] = jnp.zeros((1, 32, chans), BF16)
    tile[33:34] = jnp.zeros((1, 32, chans), BF16)

    reduced = dot(result, box_reduce[...])
    pairs = reduced + pltpu.roll(reduced, 1023, 0)
    quads = (pairs + pltpu.roll(pairs, 1024 - 32, 0)) * 0.25
    pooled[...] = quads.astype(BF16).astype(F32).reshape(32, 32, quads.shape[1])

    copies[0].wait()
    out_chans = first_w.shape[2]

    def first_rows(q, carry):
        cols = []
        for i in range(3):
            lhs = tile[pl.ds(q * 8 + i, 8)].reshape(256, chans)
            before, middle, after = (dot(lhs, first_w[3 * i + j]) for j in range(3))
            before = pltpu.roll(before, 1, 0)
            after = pltpu.roll(after, 255, 0)
            left = middle + after
            cols.append((left, before + left, before + middle))
        for v in range(3):
            below = cols[1][v] + cols[2][v]
            for u, value in ((0, below), (1, cols[0][v] + below), (2, cols[0][v] + cols[1][v])):
                value = jnp.maximum(value, 0).astype(BF16).astype(F32).reshape(8, 32, out_chans)
                for h in range(out_chans // 128):
                    variants[h, 3 * u + v, pl.ds(q * 8, 8), 0:32, :] = value[:, :, 128 * h : 128 * h + 128]
        return carry

    lax.fori_loop(0, 4, first_rows, 0)

    slots = anchor.shape[0] // 2
    for crop in (crop_a, crop_b):
        crop[:, 0:1] = jnp.zeros((slots, 1, 16, out_chans), BF16)
        crop[:, 15:16] = jnp.zeros((slots, 1, 16, out_chans), BF16)
    lane = lax.broadcasted_iota(jnp.int32, (8, 128), 0)

    def cut(n, carry):
        r0 = anchor[2 * n]
        c0 = anchor[2 * n + 1]
        for r in range(CROP):
            u = 0 if r == 0 else (2 if r == CROP - 1 else 1)
            for h in range(out_chans // 128):
                low = jnp.where(
                    lane == 0,
                    variants[h, 3 * u, r0 + r, pl.ds(c0, 8), :],
                    variants[h, 3 * u + 1, r0 + r, pl.ds(c0, 8), :],
                )
                high = jnp.where(
                    lane == 5,
                    variants[h, 3 * u + 2, r0 + r, pl.ds(c0 + 8, 8), :],
                    variants[h, 3 * u + 1, r0 + r, pl.ds(c0 + 8, 8), :],
                )
                high = jnp.where(lane < 6, high, 0.0)
                crop_a[n, r + 1, :, 128 * h : 128 * h + 128] = jnp.concatenate(
                    [low, high], axis=0
                ).astype(BF16)
        for a in range(CROP // 2):
            for b in range(CROP // 2):
                box_in[a * 7 + b, pl.ds(n, 1), :] = pooled[r0 + 2 * a, pl.ds(c0 + 2 * b, 1), :]
        return carry

    lax.fori_loop(0, slots, cut, 0)

    copies[1].wait()
    size = GROUP * CROP * 16
    inside = lax.broadcasted_iota(jnp.int32, (size, out_chans), 0) % 16 < CROP

    def layer(q, k, source):
        parts = conv_rows(
            lambda i: source[pl.ds(q * GROUP, GROUP), i : i + CROP].reshape(size, out_chans),
            lambda o: rest_w[k, o],
        )
        value = jnp.maximum(shifted(*parts), 0)
        return jnp.where(inside, value, 0.0).astype(BF16)

    def group(q, carry):
        shape = (GROUP, CROP, 16, out_chans)
        crop_b[pl.ds(q * GROUP, GROUP), 1 : CROP + 1] = layer(q, 0, crop_a).reshape(shape)
        crop_a[pl.ds(q * GROUP, GROUP), 1 : CROP + 1] = layer(q, 1, crop_b).reshape(shape)
        last = layer(q, 2, crop_a)
        out_logits[q] = lax.dot_general(
            logit_w[...], last, (((1,), (1,)), ((), ())), preferred_element_type=F32
        )
        return carry

    lax.fori_loop(0, slots // GROUP, group, 0)

    copies[2].wait()
    copies[3].wait()
    box_sum[...] = jnp.zeros_like(box_sum)
    depth = 7 * box_in.shape[2]

    def hidden(a, carry):
        lhs = jnp.concatenate([box_in[a * 7 + b].astype(BF16) for b in range(7)], axis=1)
        box_sum[...] += dot(lhs, hidden_w[pl.ds(pl.multiple_of(a * depth, 128), depth), :])
        return carry

    lax.fori_loop(0, 7, hidden, 0)
    box_first = jnp.maximum(box_sum[...], 0).astype(BF16)
    box_next = jnp.maximum(dot(box_first, second_w[...]), 0).astype(BF16)
    out_scores[...] = dot(box_next, predict_w[...])


def on_device(
    rows_total,
    cols_total,
    features,
    block_reduce,
    block_spatial,
    block_expand,
    mask_first,
    mask_rest,
    mask_logit,
    box_reduce,
    box_hidden,
    box_second,
    box_predict,
    roi_anchor,
    roi_dest,
    roi_slot,
):
    chans = features.shape[2]
    slots = roi_anchor.shape[2]
    flat = features.reshape(-1, chans)
    edges = exchange(flat, rows_total, cols_total)
    inner_w = block_reduce.shape[2]
    mask_w = mask_first.shape[2]
    box_w = box_reduce.shape[1]
    hidden = box_hidden.shape[1]
    lanes = GROUP * CROP * 16
    vmem = pl.BlockSpec(memory_space=pltpu.VMEM)
    hbm = pl.BlockSpec(memory_space=pl.ANY)
    smem = pl.BlockSpec(memory_space=pltpu.SMEM)
    result, logits, scores = pl.pallas_call(
        lambda *refs: main_kernel(rows_total, cols_total, *refs),
        out_shape=(
            jax.ShapeDtypeStruct(flat.shape, BF16),
            jax.ShapeDtypeStruct((slots // GROUP, 8, lanes), F32),
            jax.ShapeDtypeStruct((slots, box_predict.shape[1]), F32),
        ),
        in_specs=[smem, vmem, vmem, vmem, vmem, vmem, vmem, hbm, hbm, vmem, vmem, hbm, hbm, vmem],
        out_specs=(vmem, vmem, vmem),
        scratch_shapes=[
            pltpu.VMEM(mask_first.shape, BF16),
            pltpu.VMEM(mask_rest.shape, BF16),
            pltpu.VMEM(box_hidden.shape, BF16),
            pltpu.VMEM(box_second.shape, BF16),
            pltpu.VMEM((37, WIDE, chans), BF16),
            pltpu.VMEM((37, WIDE, inner_w), BF16),
            pltpu.VMEM((35, WIDE, chans), BF16),
            pltpu.VMEM((34, 32, chans), BF16),
            pltpu.VMEM((mask_w // 128, 9, 32, 40, 128), F32),
            pltpu.VMEM((32, 32, box_w), F32),
            pltpu.VMEM((49, slots, box_w), F32),
            pltpu.VMEM((slots, hidden), F32),
            pltpu.VMEM((slots, 16, 16, mask_w), BF16),
            pltpu.VMEM((slots, 16, 16, mask_w), BF16),
            pltpu.SemaphoreType.DMA((4,)),
        ],
        compiler_params=pltpu.CompilerParams(vmem_limit_bytes=62 * 2**20),
    )(
        roi_anchor.reshape(-1),
        flat,
        edges,
        jnp.asarray(side_matrix(), BF16),
        block_reduce,
        block_spatial,
        block_expand,
        mask_first,
        mask_rest,
        jnp.broadcast_to(mask_logit[None], (8, mask_w)),
        box_reduce,
        box_hidden,
        box_second,
        box_predict,
    )
    used = roi_dest[0, 0] >= 0
    logits = logits[:, 0].reshape(slots, CROP, 16)[:, :, :CROP].reshape(slots, CROP * CROP)
    logits = jnp.where(used[:, None], logits, 0.0)
    scores = jnp.where(used[:, None], scores, 0.0)
    return (result.reshape(features.shape), logits[None, None], scores[None, None])


def solution(mesh):
    in_specs = (
        P("ty", "tx", None),
        P(),
        P(),
        P(),
        P(),
        P(),
        P(),
        P(),
        P(),
        P(),
        P(),
        P("ty", "tx", None, None),
        P("ty", "tx", None),
        P("ty", "tx", None),
    )
    out_specs = (P("ty", "tx", None), P("ty", "tx", None, None), P("ty", "tx", None, None))
    rows_total, cols_total = mesh.shape["ty"], mesh.shape["tx"]
    return jax.shard_map(
        lambda *arrays: on_device(rows_total, cols_total, *arrays),
        mesh=mesh,
        in_specs=in_specs,
        out_specs=out_specs,
        check_vma=False,
    )
```

profile of v0, /device:TPU:17, one launch (start us, length us, event | category | flops | bytes accessed | tf_op | source)
XLA Modules:
  0.0 72.6 jit_solution(702461388202045770)
XLA Ops:
  0.6 0.0 copy-start
  0.6 1.2 %copy-done = bf16[32,32,512]{2,1,0:T(8,128)(2,1)S(1)} copy-done((bf16[32,32,512]{2,1,0:T(8,128)(2,1)S(1)}, bf16[32,32,512]{2,1,0:T(8,128)(2,1)}, u32[]{:S(2)}) %copy-start) | copy-done | bytes 1048600
  1.9 0.0 copy-start.2
  1.9 1.0 %copy-done.2 = bf16[192,1024]{1,0:T(8,128)(2,1)S(1)} copy-done((bf16[192,1024]{1,0:T(8,128)(2,1)S(1)}, bf16[192,1024]{1,0:T(8,128)(2,1)}, u32[]{:S(2)}) %copy-start.2) | copy-done | bytes 393240
  2.9 8.7 %shard_map.166.refs_2_ = bf16[320,512]{1,0:T(8,128)(2,1)S(1)} custom-call(bf16[1024,512]{1,0:T(8,128)(2,1)S(1)} %bitcast.10, bf16[192,1024]{1,0:T(8,128)(2,1)S(1)} %copy-done.2), custom_call_target="tpu_custom_call" | custom-call | tf_op jit(solution)/shard_map/pallas_call | solution.py:145
  11.6 0.0 copy-start.1
  11.6 0.7 copy-done.1
  12.3 1.6 %copy.22.refs_13_ = bf16[1024,5]{1,0:T(8,128)(2,1)} copy(bf16[1024,5]{0,1:T(8,128)(2,1)} %param.26) | data formatting | bytes 20480 | tf_op args[10]
  13.9 0.8 %copy.21 = s32[1,1,32,2]{3,2,1,0:T(8,128)S(1)} copy(s32[1,1,32,2]{2,3,1,0:T(2,128)} %param.27) | data formatting | bytes 512 | tf_op args[11]
  14.7 0.6 reshape.55.refs_0_
  15.3 1.2 %broadcast_in_dim.36.refs_9_ = bf16[8,256]{1,0:T(8,128)(2,1)} broadcast(bf16[256]{0:T(256)(128)(2,1)} %param.22), dimensions={1} | broadcast | bytes 4608 | tf_op jit(solution)/shard_map/broadcast_in_dim | solution.py:443
  16.5 0.0 copy-start.3
  16.5 52.5 %shard_map.167 = (bf16[1024,512]{1,0:T(8,128)(2,1)}, f32[8,8,896]{2,1,0:T(8,128)}, f32[32,5]{1,0:T(8,128)}) custom-call(s32[64]{0:T(128)} %reshape.55.refs_0_, bf16[1024,512]{1,0:T(8,128)(2,1)} %bitcast.9, bf16[320,512]{1,0:T(8,128)(2,1)} %copy-done.1, bf16[592,320]{1,0:T(8,128)(2,1)} %constant.9.clone.refs_3_, bf16[2,512,128]{2,1,0:T(8,128)(2,1)} %refs_4_.1, ...), custom_call_target="tpu_custom_call" | custom-call | tf_op jit(solution)/shard_map/pallas_call | solution.py:406
  69.0 1.0 %slice_reduce_fusion = f32[8,896]{1,0:T(8,128)S(1)} fusion(f32[8,8,896]{2,1,0:T(8,128)} %get-tuple-element.7), kind=kLoop, calls=%fused_computation.1 | loop fusion | bytes 57344 | tf_op jit(solution)/shard_map/slice | solution.py:450
  70.0 0.1 reshape_squeeze.3
  70.2 0.1 reshape.59
  70.3 0.1 copy.26
  70.4 0.0 copy-done.3
  70.5 0.7 copy.24
  71.1 0.8 %select_bitcast_fusion = f32[1,1,32,5]{3,2,1,0:T(8,128)S(1)} fusion(f32[32,5]{1,0:T(8,128)} %get-tuple-element.8, pred[32]{0:T(512)(128)(4,1)S(1)} %compare_bitcast_fusion), kind=kLoop, calls=%fused_computation.2 | loop fusion | flops 160 | bytes 1312 | tf_op jit(solution)/shard_map/broadcast_in_dim | solution.py:453
  71.9 0.7 copy.25
  (2 shorter events, 0.0 us)
Async XLA Ops:
  0.6 1.2 %copy-start = (bf16[32,32,512]{2,1,0:T(8,128)(2,1)S(1)}, bf16[32,32,512]{2,1,0:T(8,128)(2,1)}, u32[]{:S(2)}) copy-start(bf16[32,32,512]{2,1,0:T(8,128)(2,1)} %param.16) | copy-start | bytes 3145732
  1.9 1.0 %copy-start.2 = (bf16[192,1024]{1,0:T(8,128)(2,1)S(1)}, bf16[192,1024]{1,0:T(8,128)(2,1)}, u32[]{:S(2)}) copy-start(bf16[192,1024]{1,0:T(8,128)(2,1)} %constant.8.clone.refs_1_) | copy-start | bytes 1179652
  11.6 0.7 copy-start.1
  16.5 53.9 %copy-start.3 = (s32[1,1,32]{2,1,0:T(1,128)S(1)}, s32[1,1,32]{2,1,0:T(1,128)}, u32[]{:S(2)}) copy-start(s32[1,1,32]{2,1,0:T(1,128)} %param.28) | copy-start | bytes 388
where the time goes:
time: 73 us; the launch traced here: 72.6 us
  Pallas kernels  61.2 us (84%)
  local copies, waits for them, and re-layouts  9.87 us (14%)
  other arithmetic  0.81 us (1%)
    pallas_call x1, Pallas kernels, on_device(): pl.pallas_call(lambda *refs: main_kernel(rows_total, cols_total, *refs),...  52.5 us
    pallas_call x1, Pallas kernels, exchange(): pl.pallas_call(lambda *refs: halo_kernel(rows_total, cols_total, *refs),...  8.73 us
    unnamed x12, local copies, waits for them, and re-layouts  6.63 us

commit v1 on v0

--- a/solution.py
+++ b/solution.py
@@ -53,8 +53,17 @@
     return chosen.reshape(37 * 16, EDGE_ROWS)
 
 
-def halo_kernel(rows_total, cols_total, feat, pack, edges, packed, send_sem, recv_sem):
+def halo_kernel(
+    rows_total, cols_total, feat_hbm, pack_hbm, edges, feat, pack, packed, send_sem, recv_sem, load_sem
+):
     row, col = lax.axis_index("ty"), lax.axis_index("tx")
+
+    loads = (
+        pltpu.make_async_copy(feat_hbm, feat, load_sem.at[0]),
+        pltpu.make_async_copy(pack_hbm, pack, load_sem.at[1]),
+    )
+    for load in loads:
+        load.start()
 
     def exists(step):
         down, across = step
@@ -81,6 +90,8 @@
                 barrier, inc=1, device_id=target(step), device_id_type=pl.DeviceIdType.MESH
             )
 
+    for load in loads:
+        load.wait()
     packed[...] = jnp.dot(pack[...], feat[...], preferred_element_type=F32).astype(BF16)
     pl.semaphore_wait(barrier, count)
 
@@ -126,11 +137,6 @@
         def _():
             copy_of(at).start()
 
-        @pl.when(jnp.logical_not(exists(step)))
-        def _():
-            start, size = SLOTS[at]
-            edges[pl.ds(start, size)] = jnp.zeros((size, edges.shape[1]), BF16)
-
     for at, step in enumerate(DIRS):
 
         @pl.when(exists(step))
@@ -141,19 +147,22 @@
 
 def exchange(features, rows_total, cols_total):
     chans = features.shape[1]
-    vmem = pl.BlockSpec(memory_space=pltpu.VMEM)
+    hbm = pl.BlockSpec(memory_space=pl.ANY)
     return pl.pallas_call(
         lambda *refs: halo_kernel(rows_total, cols_total, *refs),
         out_shape=jax.ShapeDtypeStruct((EDGE_ROWS, chans), BF16),
-        in_specs=[vmem, vmem],
-        out_specs=vmem,
+        in_specs=[hbm, hbm],
+        out_specs=hbm,
         scratch_shapes=[
+            pltpu.VMEM(features.shape, BF16),
+            pltpu.VMEM((192, SIDE * SIDE), BF16),
             pltpu.VMEM((192, chans), BF16),
             pltpu.SemaphoreType.DMA((8,)),
             pltpu.SemaphoreType.DMA((8,)),
+            pltpu.SemaphoreType.DMA((2,)),
         ],
         compiler_params=pltpu.CompilerParams(
-            collective_id=0, has_side_effects=True, vmem_limit_bytes=16 * 2**20
+            collective_id=0, has_side_effects=True, vmem_limit_bytes=60 * 2**20
         ),
     )(features, jnp.asarray(pack_matrix(), BF16))
 
@@ -175,31 +184,39 @@
     ]
 
 
-GROUP = 4
+GROUP = 8
 
 
 def main_kernel(
     rows_total,
     cols_total,
     anchor,
-    feat,
-    edges,
-    side,
-    reduce_w,
-    spatial_w,
-    expand_w,
+    dest,
+    dest_row,
+    feat_hbm,
+    edges_hbm,
+    side_hbm,
+    reduce_hbm,
+    spatial_hbm,
+    expand_hbm,
     first_hbm,
     rest_hbm,
     logit_w,
-    box_reduce,
+    box_reduce_hbm,
     hidden_hbm,
     second_hbm,
     predict_w,
     out_map,
     out_logits,
     out_scores,
+    edges,
+    side,
+    reduce_w,
+    spatial_w,
+    expand_w,
     first_w,
     rest_w,
+    box_reduce,
     hidden_w,
     second_w,
     wide,
@@ -210,24 +227,50 @@
     pooled,
     box_in,
     box_sum,
+    mixed_w,
     crop_a,
     crop_b,
+    raw,
     sems,
 ):
     copies = [
         pltpu.make_async_copy(source, place, sems.at[at])
         for at, (source, place) in enumerate(
-            ((first_hbm, first_w), (rest_hbm, rest_w), (hidden_hbm, hidden_w), (second_hbm, second_w))
+            (
+                (edges_hbm, edges),
+                (side_hbm, side),
+                (feat_hbm, wide.at[3:35, 0:32]),
+                (reduce_hbm, reduce_w),
+                (spatial_hbm, spatial_w),
+                (expand_hbm, expand_w),
+                (box_reduce_hbm, box_reduce),
+                (first_hbm, first_w),
+                (rest_hbm, rest_w),
+                (hidden_hbm, hidden_w),
+                (second_hbm, second_w),
+            )
         )
     ]
     for copy in copies:
         copy.start()
-    chans = feat.shape[1]
+    chans = wide.shape[2]
     row_at, col_at = lax.axis_index("ty"), lax.axis_index("tx")
+    for copy in copies[:6]:
+        copy.wait()
+
+    for (down, across), (start, size) in zip(DIRS, SLOTS):
+        gone = jnp.bool_(False)
+        if down:
+            gone = row_at == (0 if down < 0 else rows_total - 1)
+        if across:
+            gone = gone | (col_at == (0 if across < 0 else cols_total - 1))
+
+        @pl.when(gone)
+        def _():
+            edges[start : start + size] = jnp.zeros((size, chans), BF16)
 
     ring = dot(side[...], edges[...]).astype(BF16)
     wide[:, 32:48, :] = ring.reshape(37, 16, chans)
-    wide[3:35, 0:32, :] = feat[...].reshape(32, 32, chans)
     wide[0:1, 0:32, :] = jnp.zeros((1, 32, chans), BF16)
     wide[1:3, 0:32, :] = edges[0:64, :].reshape(2, 32, chans)
     wide[35:37, 0:32, :] = edges[64:128, :].reshape(2, 32, chans)
@@ -273,42 +316,43 @@
     tile[0:1] = jnp.zeros((1, 32, chans), BF16)
     tile[33:34] = jnp.zeros((1, 32, chans), BF16)
 
+    copies[6].wait()
     reduced = dot(result, box_reduce[...])
     pairs = reduced + pltpu.roll(reduced, 1023, 0)
     quads = (pairs + pltpu.roll(pairs, 1024 - 32, 0)) * 0.25
     pooled[...] = quads.astype(BF16).astype(F32).reshape(32, 32, quads.shape[1])
 
-    copies[0].wait()
+    copies[7].wait()
     out_chans = first_w.shape[2]
 
     def first_rows(q, carry):
         cols = []
         for i in range(3):
-            lhs = tile[pl.ds(q * 8 + i, 8)].reshape(256, chans)
+            lhs = tile[pl.ds(q * 16 + i, 16)].reshape(512, chans)
             before, middle, after = (dot(lhs, first_w[3 * i + j]) for j in range(3))
             before = pltpu.roll(before, 1, 0)
-            after = pltpu.roll(after, 255, 0)
+            after = pltpu.roll(after, 511, 0)
             left = middle + after
             cols.append((left, before + left, before + middle))
         for v in range(3):
             below = cols[1][v] + cols[2][v]
             for u, value in ((0, below), (1, cols[0][v] + below), (2, cols[0][v] + cols[1][v])):
-                value = jnp.maximum(value, 0).astype(BF16).astype(F32).reshape(8, 32, out_chans)
+                value = jnp.maximum(value, 0).astype(BF16).astype(F32).reshape(16, 32, out_chans)
                 for h in range(out_chans // 128):
-                    variants[h, 3 * u + v, pl.ds(q * 8, 8), 0:32, :] = value[:, :, 128 * h : 128 * h + 128]
+                    variants[h, 3 * u + v, pl.ds(q * 16, 16), 0:32, :] = value[:, :, 128 * h : 128 * h + 128]
         return carry
 
-    lax.fori_loop(0, 4, first_rows, 0)
-
-    slots = anchor.shape[0] // 2
+    lax.fori_loop(0, 2, first_rows, 0)
+
+    slots = anchor.shape[1]
     for crop in (crop_a, crop_b):
-        crop[:, 0:1] = jnp.zeros((slots, 1, 16, out_chans), BF16)
-        crop[:, 15:16] = jnp.zeros((slots, 1, 16, out_chans), BF16)
+        crop[:, 0, 0] = jnp.zeros((slots, 16, out_chans), BF16)
+        crop[:, 1, 7] = jnp.zeros((slots, 16, out_chans), BF16)
     lane = lax.broadcasted_iota(jnp.int32, (8, 128), 0)
 
     def cut(n, carry):
-        r0 = anchor[2 * n]
-        c0 = anchor[2 * n + 1]
+        r0 = anchor[0, n]
+        c0 = anchor[1, n]
         for r in range(CROP):
             u = 0 if r == 0 else (2 if r == CROP - 1 else 1)
             for h in range(out_chans // 128):
@@ -323,7 +367,7 @@
                     variants[h, 3 * u + 1, r0 + r, pl.ds(c0 + 8, 8), :],
                 )
                 high = jnp.where(lane < 6, high, 0.0)
-                crop_a[n, r + 1, :, 128 * h : 128 * h + 128] = jnp.concatenate(
+                crop_a[n, (r + 1) % 2, (r + 1) // 2, :, 128 * h : 128 * h + 128] = jnp.concatenate(
                     [low, high], axis=0
                 ).astype(BF16)
         for a in range(CROP // 2):
@@ -333,32 +377,81 @@
 
     lax.fori_loop(0, slots, cut, 0)
 
-    copies[1].wait()
-    size = GROUP * CROP * 16
+    copies[8].wait()
+
+    def mix(at, carry):
+        k, j = at // 3, at % 3
+        ends = (rest_w[k, j].astype(F32) + rest_w[k, 6 + j].astype(F32)) * 0.5
+        centre = rest_w[k, 3 + j].astype(F32) * 0.5
+        mixed_w[at, 0] = (ends + centre).astype(BF16)
+        mixed_w[at, 1] = (ends - centre).astype(BF16)
+        return carry
+
+    lax.fori_loop(0, 9, mix, 0)
+
+    size = GROUP * (CROP // 2) * 16
     inside = lax.broadcasted_iota(jnp.int32, (size, out_chans), 0) % 16 < CROP
 
     def layer(q, k, source):
-        parts = conv_rows(
-            lambda i: source[pl.ds(q * GROUP, GROUP), i : i + CROP].reshape(size, out_chans),
-            lambda o: rest_w[k, o],
+        some = pl.ds(q * GROUP, GROUP)
+        shape = (size, out_chans)
+        d0, d2 = source[some, 0, 0:7].reshape(shape), source[some, 0, 1:8].reshape(shape)
+        d1, d3 = source[some, 1, 0:7].reshape(shape), source[some, 1, 1:8].reshape(shape)
+        u0, u1, u2, u3 = d0 - d2, d1 + d2, d2 - d1, d1 - d3
+        even, odd = [], []
+        for j in range(3):
+            m0 = dot(u0, rest_w[k, j])
+            m1 = dot(u1, mixed_w[3 * k + j, 0])
+            m2 = dot(u2, mixed_w[3 * k + j, 1])
+            m3 = dot(u3, rest_w[k, 6 + j])
+            even.append(m0 + m1 + m2)
+            odd.append(m1 - m2 - m3)
+        return [
+            jnp.where(inside, jnp.maximum(shifted(*parts), 0), 0.0).astype(BF16)
+            for parts in (even, odd)
+        ]
+
+    def group(q, carry):
+        shape = (GROUP, CROP // 2, 16, out_chans)
+        some = pl.ds(q * GROUP, GROUP)
+        for k, (source, place) in enumerate(((crop_a, crop_b), (crop_b, crop_a))):
+            even, odd = layer(q, k, source)
+            place[some, 1, 0:7] = even.reshape(shape)
+            place[some, 0, 1:8] = odd.reshape(shape)
+        each = (CROP // 2) * 16
+        query = jnp.broadcast_to(logit_w[...], (8, out_chans))
+        for side_at, last in enumerate(layer(q, 2, crop_a)):
+            for g in range(GROUP):
+                line = lax.dot_general(
+                    query,
+                    last[g * each : (g + 1) * each],
+                    (((1,), (1,)), ((), ())),
+                    preferred_element_type=F32,
+                )
+                used = dest[0, q * GROUP + g] >= 0
+                raw[side_at, q * GROUP + g] = jnp.where(used, line, 0.0)
+        return carry
+
+    lax.fori_loop(0, slots // GROUP, group, 0)
+
+    each = (CROP // 2) * 16
+    a_at = lax.broadcasted_iota(jnp.int32, (each, CROP * CROP), 0)
+    b_at = lax.broadcasted_iota(jnp.int32, (each, CROP * CROP), 1)
+    t_at, c_at = a_at // 16, a_at % 16
+    logits = None
+    for side_at in range(2):
+        chosen = (b_at == (2 * t_at + side_at) * CROP + c_at) & (c_at < CROP)
+        term = jnp.dot(
+            raw[side_at, :, 0, :],
+            chosen.astype(F32),
+            precision=lax.Precision.HIGHEST,
+            preferred_element_type=F32,
         )
-        value = jnp.maximum(shifted(*parts), 0)
-        return jnp.where(inside, value, 0.0).astype(BF16)
-
-    def group(q, carry):
-        shape = (GROUP, CROP, 16, out_chans)
-        crop_b[pl.ds(q * GROUP, GROUP), 1 : CROP + 1] = layer(q, 0, crop_a).reshape(shape)
-        crop_a[pl.ds(q * GROUP, GROUP), 1 : CROP + 1] = layer(q, 1, crop_b).reshape(shape)
-        last = layer(q, 2, crop_a)
-        out_logits[q] = lax.dot_general(
-            logit_w[...], last, (((1,), (1,)), ((), ())), preferred_element_type=F32
-        )
-        return carry
-
-    lax.fori_loop(0, slots // GROUP, group, 0)
-
-    copies[2].wait()
-    copies[3].wait()
+        logits = term if logits is None else logits + term
+    out_logits[...] = logits
+
+    copies[9].wait()
+    copies[10].wait()
     box_sum[...] = jnp.zeros_like(box_sum)
     depth = 7 * box_in.shape[2]
 
@@ -370,7 +463,11 @@
     lax.fori_loop(0, 7, hidden, 0)
     box_first = jnp.maximum(box_sum[...], 0).astype(BF16)
     box_next = jnp.maximum(dot(box_first, second_w[...]), 0).astype(BF16)
-    out_scores[...] = dot(box_next, predict_w[...])
+    scores = lax.dot_general(
+        predict_w[...], box_next, (((1,), (1,)), ((), ())), preferred_element_type=F32
+    )
+    scores = jnp.where(dest_row[...] >= 0, scores, 0.0)
+    out_scores[...] = scores.reshape(out_scores.shape)
 
 
 def on_device(
@@ -399,22 +496,29 @@
     mask_w = mask_first.shape[2]
     box_w = box_reduce.shape[1]
     hidden = box_hidden.shape[1]
-    lanes = GROUP * CROP * 16
+    outputs = box_predict.shape[1]
     vmem = pl.BlockSpec(memory_space=pltpu.VMEM)
     hbm = pl.BlockSpec(memory_space=pl.ANY)
     smem = pl.BlockSpec(memory_space=pltpu.SMEM)
+    side = side_matrix()
     result, logits, scores = pl.pallas_call(
         lambda *refs: main_kernel(rows_total, cols_total, *refs),
         out_shape=(
             jax.ShapeDtypeStruct(flat.shape, BF16),
-            jax.ShapeDtypeStruct((slots // GROUP, 8, lanes), F32),
-            jax.ShapeDtypeStruct((slots, box_predict.shape[1]), F32),
+            jax.ShapeDtypeStruct((slots, CROP * CROP), F32),
+            jax.ShapeDtypeStruct((outputs, 1, slots), F32),
         ),
-        in_specs=[smem, vmem, vmem, vmem, vmem, vmem, vmem, hbm, hbm, vmem, vmem, hbm, hbm, vmem],
+        in_specs=[smem, smem, vmem] + [hbm] * 8 + [vmem] + [hbm] * 3 + [vmem],
         out_specs=(vmem, vmem, vmem),
         scratch_shapes=[
+            pltpu.VMEM(edges.shape, BF16),
+            pltpu.VMEM(side.shape, BF16),
+            pltpu.VMEM(block_reduce.shape, BF16),
+            pltpu.VMEM(block_spatial.shape, BF16),
+            pltpu.VMEM(block_expand.shape, BF16),
             pltpu.VMEM(mask_first.shape, BF16),
             pltpu.VMEM(mask_rest.shape, BF16),
+            pltpu.VMEM(box_reduce.shape, BF16),
             pltpu.VMEM(box_hidden.shape, BF16),
             pltpu.VMEM(box_second.shape, BF16),
             pltpu.VMEM((37, WIDE, chans), BF16),
@@ -425,32 +529,33 @@
             pltpu.VMEM((32, 32, box_w), F32),
             pltpu.VMEM((49, slots, box_w), F32),
             pltpu.VMEM((slots, hidden), F32),
-            pltpu.VMEM((slots, 16, 16, mask_w), BF16),
-            pltpu.VMEM((slots, 16, 16, mask_w), BF16),
-            pltpu.SemaphoreType.DMA((4,)),
+            pltpu.VMEM((9, 2, mask_w, mask_w), BF16),
+            pltpu.VMEM((slots, 2, 8, 16, mask_w), BF16),
+            pltpu.VMEM((slots, 2, 8, 16, mask_w), BF16),
+            pltpu.VMEM((2, slots, 8, (CROP // 2) * 16), F32),
+            pltpu.SemaphoreType.DMA((11,)),
         ],
-        compiler_params=pltpu.CompilerParams(vmem_limit_bytes=62 * 2**20),
+        compiler_params=pltpu.CompilerParams(vmem_limit_bytes=63 * 2**20),
     )(
-        roi_anchor.reshape(-1),
-        flat,
+        roi_anchor[0, 0].T,
+        roi_dest[0],
+        roi_dest[0],
+        features,
         edges,
-        jnp.asarray(side_matrix(), BF16),
+        jnp.asarray(side, BF16),
         block_reduce,
         block_spatial,
         block_expand,
         mask_first,
         mask_rest,
-        jnp.broadcast_to(mask_logit[None], (8, mask_w)),
+        mask_logit[None],
         box_reduce,
         box_hidden,
         box_second,
-        box_predict,
-    )
-    used = roi_dest[0, 0] >= 0
-    logits = logits[:, 0].reshape(slots, CROP, 16)[:, :, :CROP].reshape(slots, CROP * CROP)
-    logits = jnp.where(used[:, None], logits, 0.0)
-    scores = jnp.where(used[:, None], scores, 0.0)
-    return (result.reshape(features.shape), logits[None, None], scores[None, None])
+        box_predict.T,
+    )
+    scores = scores.transpose(1, 2, 0)[None]
+    return (result.reshape(features.shape), logits[None, None], scores)
 
 
 def solution(mesh):

time: 73 us -> 56.3 us (0.77)
  local copies, waits for them, and re-layouts: 9.87 us -> 1.25 us
  Pallas kernels: 61.2 us -> 54 us
  other arithmetic: 0.81 us -> 0 us
    pallas_call x1, Pallas kernels: 52.5 us -> 44.9 us  [on_device(): pl.pallas_call(lambda *refs: main_kernel(rows_total, cols_total, *refs),...]
    unnamed x12 -> x0, local copies, waits for them, and re-layouts: 6.63 us -> none
    slice x1 -> x0, local copies, waits for them, and re-layouts: 1.01 us -> none  [on_device(): logits[:, 0].reshape(slots, CROP, 16)[:, :, :CROP]]
    reshape x3 -> x0, local copies, waits for them, and re-layouts: 0.86 us -> none  [the longest x1 0.62 us: on_device(): roi_anchor.reshape(-1)]
    broadcast_in_dim x1 -> x0, other arithmetic: 0.79 us -> none  [on_device(): scores[None, None]]
where the time goes in v1:
time: 56.3 us; the launch traced here: 56.1 us
  Pallas kernels  54 us (96%)
  local copies, waits for them, and re-layouts  1.25 us (2%)
  between operations  0.8 us (1%)
    pallas_call x1, Pallas kernels, on_device(): pl.pallas_call(lambda *refs: main_kernel(rows_total, cols_total, *refs),...  44.9 us
    pallas_call x1, Pallas kernels, exchange(): pl.pallas_call(lambda *refs: halo_kernel(rows_total, cols_total, *refs),...  9.07 us
    broadcast_in_dim x1, local copies, waits for them, and re-layouts, on_device(): mask_logit[None]  1.25 us

profile of v1, /device:TPU:17, one launch (start us, length us, event | category | flops | bytes accessed | tf_op | source)
XLA Modules:
  0.0 56.1 jit_solution(16464233210776943782)
XLA Ops:
  0.6 1.2 %broadcast_in_dim.9.refs_11_ = bf16[1,256]{1,0:T(2,128)(2,1)} reshape(bf16[256]{0:T(256)(128)(2,1)} %param.22) | data formatting | bytes 1024 | tf_op jit(solution)/shard_map/broadcast_in_dim | solution.py:551
  1.9 9.1 %shard_map.166.refs_4_ = bf16[320,512]{1,0:T(8,128)(2,1)} custom-call(bf16[1024,512]{1,0:T(8,128)(2,1)} %bitcast.13, bf16[192,1024]{1,0:T(8,128)(2,1)} %constant.4.clone.refs_1_), custom_call_target="tpu_custom_call" | custom-call | tf_op jit(solution)/shard_map/pallas_call | solution.py:151
  11.0 44.9 %shard_map.167 = (bf16[1024,512]{1,0:T(8,128)(2,1)}, f32[32,196]{1,0:T(8,128)}, f32[5,1,32]{2,1,0:T(1,128)}) custom-call(s32[2,32]{1,0:T(2,128)} %bitcast.17, s32[1,32]{1,0:T(1,128)} %bitcast.15, s32[1,32]{1,0:T(1,128)} %bitcast.16, bf16[32,32,512]{2,1,0:T(8,128)(2,1)} %refs_3_.1, bf16[320,512]{1,0:T(8,128)(2,1)} %shard_map.166.refs_4_, ...), custom_call_target="tpu_custom_call" | custom-call | tf_op jit(solution)/shard_map/pallas_call | solution.py:504

commit v2 on v1

--- a/solution.py
+++ b/solution.py
@@ -251,12 +251,14 @@
             )
         )
     ]
-    for copy in copies:
+    for copy in copies[:7]:
         copy.start()
     chans = wide.shape[2]
     row_at, col_at = lax.axis_index("ty"), lax.axis_index("tx")
     for copy in copies[:6]:
         copy.wait()
+    for copy in copies[7:]:
+        copy.start()
 
     for (down, across), (start, size) in zip(DIRS, SLOTS):
         gone = jnp.bool_(False)
@@ -346,11 +348,11 @@
 
     slots = anchor.shape[1]
     for crop in (crop_a, crop_b):
-        crop[:, 0, 0] = jnp.zeros((slots, 16, out_chans), BF16)
-        crop[:, 1, 7] = jnp.zeros((slots, 16, out_chans), BF16)
+        crop[:, 0, 0] = jnp.zeros((GROUP, 16, 3 * out_chans), BF16)
+        crop[:, 1, 7] = jnp.zeros((GROUP, 16, 3 * out_chans), BF16)
     lane = lax.broadcasted_iota(jnp.int32, (8, 128), 0)
 
-    def cut(n, carry):
+    def cut(n, g):
         r0 = anchor[0, n]
         c0 = anchor[1, n]
         for r in range(CROP):
@@ -367,15 +369,13 @@
                     variants[h, 3 * u + 1, r0 + r, pl.ds(c0 + 8, 8), :],
                 )
                 high = jnp.where(lane < 6, high, 0.0)
-                crop_a[n, (r + 1) % 2, (r + 1) // 2, :, 128 * h : 128 * h + 128] = jnp.concatenate(
-                    [low, high], axis=0
-                ).astype(BF16)
+                cells = jnp.concatenate([low, high], axis=0)
+                for at, moved in enumerate((pltpu.roll(cells, 1, 0), cells, pltpu.roll(cells, 15, 0))):
+                    first = at * out_chans + 128 * h
+                    crop_a[g, (r + 1) % 2, (r + 1) // 2, :, first : first + 128] = moved.astype(BF16)
         for a in range(CROP // 2):
             for b in range(CROP // 2):
                 box_in[a * 7 + b, pl.ds(n, 1), :] = pooled[r0 + 2 * a, pl.ds(c0 + 2 * b, 1), :]
-        return carry
-
-    lax.fori_loop(0, slots, cut, 0)
 
     copies[8].wait()
 
@@ -383,8 +383,8 @@
         k, j = at // 3, at % 3
         ends = (rest_w[k, j].astype(F32) + rest_w[k, 6 + j].astype(F32)) * 0.5
         centre = rest_w[k, 3 + j].astype(F32) * 0.5
-        mixed_w[at, 0] = (ends + centre).astype(BF16)
-        mixed_w[at, 1] = (ends - centre).astype(BF16)
+        mixed_w[k, 0, j] = (ends + centre).astype(BF16)
+        mixed_w[k, 1, j] = (ends - centre).astype(BF16)
         return carry
 
     lax.fori_loop(0, 9, mix, 0)
@@ -392,35 +392,36 @@
     size = GROUP * (CROP // 2) * 16
     inside = lax.broadcasted_iota(jnp.int32, (size, out_chans), 0) % 16 < CROP
 
-    def layer(q, k, source):
-        some = pl.ds(q * GROUP, GROUP)
-        shape = (size, out_chans)
-        d0, d2 = source[some, 0, 0:7].reshape(shape), source[some, 0, 1:8].reshape(shape)
-        d1, d3 = source[some, 1, 0:7].reshape(shape), source[some, 1, 1:8].reshape(shape)
-        u0, u1, u2, u3 = d0 - d2, d1 + d2, d2 - d1, d1 - d3
-        even, odd = [], []
-        for j in range(3):
-            m0 = dot(u0, rest_w[k, j])
-            m1 = dot(u1, mixed_w[3 * k + j, 0])
-            m2 = dot(u2, mixed_w[3 * k + j, 1])
-            m3 = dot(u3, rest_w[k, 6 + j])
-            even.append(m0 + m1 + m2)
-            odd.append(m1 - m2 - m3)
-        return [
-            jnp.where(inside, jnp.maximum(shifted(*parts), 0), 0.0).astype(BF16)
-            for parts in (even, odd)
-        ]
+    def layer(k, source):
+        depth = 3 * out_chans
+        shape, across = (size, depth), (depth, out_chans)
+        d0, d2 = source[:, 0, 0:7].reshape(shape), source[:, 0, 1:8].reshape(shape)
+        d1, d3 = source[:, 1, 0:7].reshape(shape), source[:, 1, 1:8].reshape(shape)
+        m1 = dot(d1 + d2, mixed_w[k, 0].reshape(across))
+        m2 = dot(d2 - d1, mixed_w[k, 1].reshape(across))
+        even = dot(d0 - d2, rest_w[k, 0:3].reshape(across)) + (m1 + m2)
+        odd = (m1 - m2) - dot(d1 - d3, rest_w[k, 6:9].reshape(across))
+        return [jnp.where(inside, jnp.maximum(value, 0), 0.0) for value in (even, odd)]
+
+    def spread(value):
+        moved = (pltpu.roll(value, 1, 0), value, pltpu.roll(value, size - 1, 0))
+        joined = jnp.concatenate([part.astype(BF16) for part in moved], axis=1)
+        return joined.reshape(GROUP, CROP // 2, 16, 3 * out_chans)
 
     def group(q, carry):
-        shape = (GROUP, CROP // 2, 16, out_chans)
-        some = pl.ds(q * GROUP, GROUP)
+        def one(g, inner_carry):
+            cut(q * GROUP + g, g)
+            return inner_carry
+
+        lax.fori_loop(0, GROUP, one, 0)
         for k, (source, place) in enumerate(((crop_a, crop_b), (crop_b, crop_a))):
-            even, odd = layer(q, k, source)
-            place[some, 1, 0:7] = even.reshape(shape)
-            place[some, 0, 1:8] = odd.reshape(shape)
+            even, odd = layer(k, source)
+            place[:, 1, 0:7] = spread(even)
+            place[:, 0, 1:8] = spread(odd)
         each = (CROP // 2) * 16
-        query = jnp.broadcast_to(logit_w[...], (8, out_chans))
-        for side_at, last in enumerate(layer(q, 2, crop_a)):
+        query = jnp.broadcast_to(logit_w[...].reshape(1, out_chans), (8, out_chans))
+        for side_at, last in enumerate(layer(2, crop_a)):
+            last = last.astype(BF16)
             for g in range(GROUP):
                 line = lax.dot_general(
                     query,
@@ -529,9 +530,9 @@
             pltpu.VMEM((32, 32, box_w), F32),
             pltpu.VMEM((49, slots, box_w), F32),
             pltpu.VMEM((slots, hidden), F32),
-            pltpu.VMEM((9, 2, mask_w, mask_w), BF16),
-            pltpu.VMEM((slots, 2, 8, 16, mask_w), BF16),
-            pltpu.VMEM((slots, 2, 8, 16, mask_w), BF16),
+            pltpu.VMEM((3, 2, 3, mask_w, mask_w), BF16),
+            pltpu.VMEM((GROUP, 2, 8, 16, 3 * mask_w), BF16),
+            pltpu.VMEM((GROUP, 2, 8, 16, 3 * mask_w), BF16),
             pltpu.VMEM((2, slots, 8, (CROP // 2) * 16), F32),
             pltpu.SemaphoreType.DMA((11,)),
         ],
@@ -548,7 +549,7 @@
         block_expand,
         mask_first,
         mask_rest,
-        mask_logit[None],
+        mask_logit,
         box_reduce,
         box_hidden,
         box_second,

time: 56.3 us -> 55.7 us (0.989)
  local copies, waits for them, and re-layouts: 1.25 us -> 0 us
  Pallas kernels: 54 us -> 54.7 us
    broadcast_in_dim x1 -> x0, local copies, waits for them, and re-layouts: 1.25 us -> none  [on_device(): mask_logit[None]]
    pallas_call x1, Pallas kernels: 44.9 us -> 45.6 us  [on_device(): pl.pallas_call(lambda *refs: main_kernel(rows_total, cols_total, *refs),...]
where the time goes in v2:
time: 55.7 us; the launch traced here: 55.5 us
  Pallas kernels  54.7 us (98%)
  between operations  0.8 us (1%)
    pallas_call x1, Pallas kernels, on_device(): pl.pallas_call(lambda *refs: main_kernel(rows_total, cols_total, *refs),...  45.6 us
    pallas_call x1, Pallas kernels, exchange(): pl.pallas_call(lambda *refs: halo_kernel(rows_total, cols_total, *refs),...  9.09 us

profile of v2, /device:TPU:17, one launch (start us, length us, event | category | flops | bytes accessed | tf_op | source)
XLA Modules:
  0.0 55.5 jit_solution(2194268913240563237)
XLA Ops:
  0.6 9.1 %shard_map.166.refs_4_ = bf16[320,512]{1,0:T(8,128)(2,1)} custom-call(bf16[1024,512]{1,0:T(8,128)(2,1)} %bitcast.13, bf16[192,1024]{1,0:T(8,128)(2,1)} %constant.4.clone.refs_1_), custom_call_target="tpu_custom_call" | custom-call | tf_op jit(solution)/shard_map/pallas_call | solution.py:151
  9.7 45.6 %shard_map.167 = (bf16[1024,512]{1,0:T(8,128)(2,1)}, f32[32,196]{1,0:T(8,128)}, f32[5,1,32]{2,1,0:T(1,128)}) custom-call(s32[2,32]{1,0:T(2,128)} %bitcast.17, s32[1,32]{1,0:T(1,128)} %bitcast.15, s32[1,32]{1,0:T(1,128)} %bitcast.16, bf16[32,32,512]{2,1,0:T(8,128)(2,1)} %refs_3_.1, bf16[320,512]{1,0:T(8,128)(2,1)} %shard_map.166.refs_4_, ...), custom_call_target="tpu_custom_call" | custom-call | tf_op jit(solution)/shard_map/pallas_call | solution.py:505
